TPU v7x, 32 devices: a whole 2x2x4 slice. The times are simulated.
32 devices in a mesh: az: 4 (over y, x), col: 8 (over z, core).
Axes of the slice: x: 2, y: 2, z: 4, core: 2. Of those that a mesh axis runs over, the one named last changes fastest.
Arguments:
- phase_field: float32 [64, 1024, 2048], P(None, 'col', 'az'), may hold values from -1 to 1
- velocity: bfloat16 [2, 64, 1024, 2048], P(None, None, 'col', 'az'), may hold values from -4 to 4
- owned_modes: int32 [32, 16], replicated, may hold values from 0 to 511, as said below
- legendre: bfloat16 [512, 1024, 512], P(('az', 'col')), as said below
- radial_inverse: bfloat16 [512, 64, 64], replicated, as said below
Outputs:
- new_phase: float32 [64, 1024, 2048], P(None, 'col', 'az')
Inputs may be any that keep to these rules, and one draw needn't show every extreme that they name: `owned_modes`: every order from 0 to 511 appears exactly once; the second half of each row is 511 minus its first half. legendre[q, t, l] is the orthonormal associated Legendre function of degree l and order m_q (owned_modes flattened at q) at cos(theta_t), normalized so that the integral of its square times sin(theta) over theta is 1, rounded to bfloat16; it is 0 for l < m_q. `radial_inverse`: one matrix for each degree.
All inputs are finite; a program needn't handle non-finite values.
Results may differ from a plain program's by a relative error of at most 0.0003.
Values sent between devices are 32-bit elements; how exact they have to be, the bound alone decides.
A program may use at most 256 MiB of HBM per device.

v0:
```python
import math

import jax
import jax.numpy as jnp
from jax import lax
from jax.sharding import PartitionSpec as P

step_time = 0.002
mobility_step = 4e-06
highest_precision = lax.Precision.HIGHEST


def padded_2(block, sides, width):
    for axis, dim in sides:
        count = lax.axis_size(axis)
        forward = [(i, i + 1) for i in range(count - 1)]
        forward.append((count - 1, 0))
        backward = [(target, source) for source, target in forward]
        low = lax.ppermute(
            lax.slice_in_dim(block, block.shape[dim] - width, None, axis=dim), axis, forward
        )
        high = lax.ppermute(lax.slice_in_dim(block, 0, width, axis=dim), axis, backward)
        block = jnp.concatenate([low, block, high], axis=dim)
    return block


def shell_radii(shells):
    return 0.75 + 0.25 * (jnp.arange(shells, dtype=jnp.float32) + 0.5) / shells


def colat_weights(count):
    row_index = jnp.arange(count, dtype=jnp.int32)
    waves = jnp.arange(1, count // 2 + 1, dtype=jnp.int32)
    turns = (2 * row_index[:, None] + 1) * waves[None, :] % (2 * count)
    cosines = jnp.cos(turns.astype(jnp.float32) * (math.pi / count))
    wave_float = waves.astype(jnp.float32)
    coefs = 1.0 / (4.0 * wave_float * wave_float - 1.0)
    return 2.0 / count * (1.0 - 2.0 * jnp.dot(cosines, coefs, precision=highest_precision))


def forward_waves(phi_index, mode_list, phi_count):
    turns = phi_index[:, None] * mode_list[None, :] % phi_count
    angle = turns.astype(jnp.float32) * (2.0 * math.pi / phi_count)
    return jnp.stack([jnp.cos(angle), -jnp.sin(angle)], axis=1) / phi_count


def inverse_waves(mode_list, phi_count):
    phi_index = jnp.arange(phi_count, dtype=jnp.int32)
    turns = mode_list[:, None] * phi_index[None, :] % phi_count
    angle = turns.astype(jnp.float32) * (2.0 * math.pi / phi_count)
    doubling = jnp.where(mode_list == 0, 1.0, 2.0).astype(jnp.float32)[:, None]
    return jnp.stack([doubling * jnp.cos(angle), -doubling * jnp.sin(angle)], axis=0)


def body(phase_field, velocity, owned_modes, legendre, radial_inverse):
    shells, theta_local, phi_local = phase_field.shape
    az_count = lax.axis_size("az")
    col_count = lax.axis_size("col")
    phi_count = phi_local * az_count
    theta_count = theta_local * col_count
    theta_block = theta_local // az_count
    mode_list = owned_modes.reshape(-1)
    mode_count = mode_list.shape[0]
    mode_dev = legendre.shape[0]
    degree_count = legendre.shape[2]
    legendre_full = legendre.astype(jnp.float32)
    shell_radius = shell_radii(shells)
    padded = padded_2(phase_field, (("az", 2), ("col", 1)), 1)
    col_here = lax.axis_index("col")
    row_index = jnp.arange(theta_local + 2, dtype=jnp.int32)
    row_mask = jnp.logical_not(
        jnp.logical_or(
            jnp.logical_and(row_index == 0, col_here == 0),
            jnp.logical_and(row_index == theta_local + 1, col_here == col_count - 1),
        )
    )
    padded = padded * row_mask.astype(jnp.float32)[None, :, None]
    centre_rows = padded[:, 1:-1, :]
    east_cell = centre_rows[:, :, 2:]
    west_cell = centre_rows[:, :, :-2]
    south_cell = padded[:, 2:, 1:-1]
    north_cell = padded[:, :-2, 1:-1]
    d_phi = (east_cell - west_cell) * (phi_count / (4.0 * math.pi))
    d_theta = (south_cell - north_cell) * (theta_count / (2.0 * math.pi))
    spin_rate = velocity[0].astype(jnp.float32)
    sweep_speed = velocity[1].astype(jnp.float32)
    advected = phase_field - step_time * (
        spin_rate * d_phi + sweep_speed / shell_radius[:, None, None] * d_theta
    )
    potential = phase_field * phase_field * phase_field - phase_field
    fields = jnp.stack([advected, potential])
    wave_table = forward_waves(jnp.arange(phi_count, dtype=jnp.int32), mode_list, phi_count)
    spectra = jnp.einsum(
        "frtp,pqk->ktqfr",
        lax.all_to_all(fields, "az", split_axis=2, concat_axis=3, tiled=True),
        wave_table,
        precision=highest_precision,
    )
    spectra = spectra.reshape(mode_count, theta_block, 4 * shells)
    gathered = lax.all_to_all(spectra, ("az", "col"), split_axis=0, concat_axis=1, tiled=True)
    gathered = gathered.reshape(mode_dev, az_count, col_count, theta_block, 4 * shells)
    gathered = jnp.transpose(gathered, (0, 2, 1, 3, 4))
    gathered = gathered.reshape(mode_dev, theta_count, 4 * shells)
    weights = colat_weights(theta_count)
    weighted = gathered * weights[None, :, None]
    coeffs = jnp.einsum("ktx,ktl->klx", weighted, legendre_full, precision=highest_precision)
    coeffs = coeffs.reshape(mode_dev, degree_count, 2, 2, shells)
    degrees = jnp.arange(degree_count, dtype=jnp.float32)
    factor = (
        mobility_step
        * (degrees * (degrees + 1.0))[:, None]
        / (shell_radius * shell_radius)[None, :]
    )
    right_side = coeffs[:, :, :, 0, :] - factor[None, :, None, :] * coeffs[:, :, :, 1, :]
    solved = jnp.einsum(
        "lrs,klqs->klqr",
        radial_inverse.astype(jnp.float32),
        right_side,
        precision=highest_precision,
    )
    synthesis = jnp.einsum(
        "ktl,klx->ktx",
        legendre_full,
        solved.reshape(mode_dev, degree_count, 2 * shells),
        precision=highest_precision,
    )
    synthesis = synthesis.reshape(mode_dev, col_count, az_count, theta_block, 2 * shells)
    synthesis = jnp.transpose(synthesis, (0, 2, 1, 3, 4)).reshape(mode_dev, theta_count, 2 * shells)
    grid_modes = lax.all_to_all(synthesis, ("az", "col"), split_axis=1, concat_axis=0, tiled=True)
    grid_modes = grid_modes.reshape(mode_count, theta_block, 2, shells)
    inverse_table = inverse_waves(mode_list, phi_count)
    row_fields = jnp.einsum("ktqr,qkp->rtp", grid_modes, inverse_table, precision=highest_precision)
    new_phase = lax.all_to_all(row_fields, "az", split_axis=2, concat_axis=1, tiled=True)
    return new_phase


def solution(mesh):
    in_specs = (
        P(None, "col", "az"),
        P(None, None, "col", "az"),
        P(),
        P(("az", "col"), None, None),
        P(),
    )
    out_specs = P(None, "col", "az")
    return jax.shard_map(body, mesh=mesh, in_specs=in_specs, out_specs=out_specs, check_vma=False)
```

profile of v0, /device:TPU:0, one launch (start us, length us, event | category | flops | bytes accessed | tf_op | source)
XLA Modules:
  0.0 1941.1 jit_solution(2712956421081684860)
XLA Ops:
  29.4 17.8 copy.50
  64.0 20.8 %maximum_multiply_fusion = f32[64,130,514]{2,0,1:T(8,128)} fusion(f32[64,1,514]{2,0,1:T(8,128)S(1)} %collective-permute-done.3, f32[64,128,1]{2,0,1:T(8,128)} %copy.48, f32[64,128,512]{2,0,1:T(8,128)} %copy.50, f32[64,128,1]{2,0,1:T(8,128)} %copy.46, f32[64,1,514]{2,0,1:T(8,128)S(1)} %collective-permute-done.2, f32[130]{0:T(256)S(1)} %not_convert_fusion), kind=kLoop, calls=%fused_computation.3 | loop fusion | flops 21382400 | bytes 34212360 | tf_op jit(solution)/shard_map/mul | solution.py:77
  84.8 46.5 %fusion.6 = (f32[1,64,128,512]{3,1,0,2:T(8,128)S(1)}, f32[1,64,128,512]{3,1,0,2:T(8,128)}) fusion(f32[64,130,514]{2,0,1:T(8,128)} %maximum_multiply_fusion, bf16[1,64,128,512]{3,2,1,0:T(8,128)(2,1)} %get-tuple-element.10, bf16[1,64,128,512]{3,2,1,0:T(8,128)(2,1)} %get-tuple-element.9, f32[64]{0:T(128)S(1)} %multiply_add_fusion.1, f32[64,128,512]{2,1,0:T(8,128)} %param.5), kind=kLoop, calls=%fused_computation.11 | loop fusion | flops 62914560 | bytes 134217984 | tf_op jit(solution)/shard_map/stack | solution.py:91
  131.3 18.8 pad_maximum_fusion
  160.2 18.0 fusion.51
  178.2 344.8 %all-to-all-done = f32[2,64,128,512]{3,1,0,2:T(8,128)} async-done(((f32[2,64,128,512]{3,1,0,2:T(8,128)}), f32[2,64,128,512]{3,1,0,2:T(8,128)}, u32[]{:S(2)}, u32[]{:S(2)}) %all-to-all-start) | async-done | bytes 33554464 | tf_op jit(solution)/shard_map/all_to_all | solution.py:95
  523.0 38.0 %copy.101 = f32[2,64,4,32,512]{4,2,1,3,0:T(4,128)} copy(f32[2,64,4,32,512]{4,1,0,3,2:T(8,128)} %bitcast.6) | data formatting | bytes 67108864 | tf_op jit(solution)/shard_map/all_to_all | solution.py:95
  561.0 39.8 %reshape.403 = f32[2,64,32,2048,1]{3,1,2,0,4:T(8,128)} reshape(f32[2,64,32,4,512]{4,3,1,2,0:T(4,128)} %bitcast.106) | data formatting | bytes 67108864 | tf_op jit(solution)/shard_map/all_to_all | solution.py:95
  600.8 112.7 %fusion.22 = f32[512,32,2,2,64]{0,4,1,3,2:T(8,128)} fusion(f32[2,64,32,2048,1]{3,1,2,0,4:T(8,128)} %reshape.403, f32[2048,1,512]{2,0,1:T(8,128)} %get-tuple-element.20, f32[2048,1,512]{2,0,1:T(8,128)} %get-tuple-element.19), kind=kOutput, calls=%fused_computation.33 | convolution fusion | flops 103083409408 | bytes 58720256 | tf_op jit(solution)/shard_map/frtp,pqk->ktqfr/dot_general | solution.py:93
  725.6 19.8 %copy.57 = f32[512,32,256]{2,1,0:T(8,128)} copy(f32[512,32,256]{0,2,1:T(8,128)} %bitcast.107) | data formatting | bytes 33554432 | tf_op jit(solution)/shard_map/reshape | solution.py:99
  772.4 341.6 %all-to-all-done.1 = f32[512,32,256]{2,1,0:T(8,128)} async-done(((f32[512,32,256]{2,1,0:T(8,128)}), f32[512,32,256]{2,1,0:T(8,128)}, u32[]{:S(2)}, u32[]{:S(2)}) %all-to-all-start.1) | async-done | bytes 16777248 | tf_op jit(solution)/shard_map/all_to_all | solution.py:100
  1127.7 27.1 %fusion.76 = f32[16,256,512]{2,1,0:T(8,128)} fusion(f32[16,1024,256]{2,1,0:T(8,128)} %bitcast_multiply_fusion, bf16[16,1024,512]{2,1,0:T(8,128)(2,1)} %param.8), kind=kOutput, calls=%fused_computation.107 | convolution fusion | flops 25769803776 | bytes 41943040 | tf_op jit(solution)/shard_map/ktx,ktl->klx/dot_general | solution.py:106
  1182.0 19.8 %fusion.42 = f32[16,512,2,64]{3,0,2,1:T(8,128)} fusion(bf16[512,64,64,1]{2,1,3,0:T(8,128)(2,1)} %copy.75, f32[16,512,2,1,64]{4,0,2,1,3:T(8,128)} %copy.86, f32[16,512,2,1,64]{4,0,2,1,3:T(8,128)} %copy.85, f32[512,64]{1,0:T(8,128)S(1)} %broadcast_divide_fusion), kind=kOutput, calls=%fused_computation.61 | convolution fusion | flops 807403520 | bytes 16908288 | tf_op jit(solution)/shard_map/lrs,klqs->klqr/dot_general | solution.py:115
  1208.7 23.3 %convolution_bitcast_fusion = f32[16,1024,128]{1,2,0:T(8,128)} fusion(f32[16,512,128]{1,2,0:T(8,128)} %bitcast.109, bf16[16,1024,512]{2,1,0:T(8,128)(2,1)} %param.8), kind=kOutput, calls=%fused_computation.62 | convolution fusion | flops 12884901888 | bytes 29360128 | tf_op jit(solution)/shard_map/ktl,klx->ktx/dot_general | solution.py:121
  1258.2 19.1 cosine_multiply_fusion
  1277.3 165.8 %all-to-all-done.2 = f32[16,1024,128]{2,0,1:T(8,128)} async-done(((f32[16,1024,128]{2,0,1:T(8,128)}), f32[16,1024,128]{2,0,1:T(8,128)}, u32[]{:S(2)}, u32[]{:S(2)}) %all-to-all-start.2) | async-done | bytes 8388640 | tf_op jit(solution)/shard_map/all_to_all | solution.py:129
  1453.1 16.9 reshape.399
  1470.0 67.6 %fusion.25 = f32[64,32,2048]{2,0,1:T(8,128)} fusion(f32[512,32,2,64]{3,2,1,0:T(2,128)} %reshape.399, f32[1,512,2048]{2,1,0:T(8,128)} %get-tuple-element.16, f32[1,512,2048]{2,1,0:T(8,128)} %get-tuple-element.15), kind=kOutput, calls=%fused_computation.34 | convolution fusion | flops 51541704704 | bytes 33554432 | tf_op jit(solution)/shard_map/ktqr,qkp->rtp/dot_general | solution.py:132
  1537.6 30.4 %copy.71 = f32[64,32,2048]{0,1,2:T(8,128)} copy(f32[64,32,2048]{2,0,1:T(8,128)} %fusion.25) | data formatting | bytes 33554432 | tf_op jit(solution)/shard_map/ktqr,qkp->rtp/transpose | solution.py:132
  1568.0 42.3 %reshape.410 = f32[4,1,1048576]{2,1,0:T(1,128)} reshape(f32[2048,32,64]{2,1,0:T(8,128)} %bitcast.104) | data formatting | bytes 33554432
  1610.3 193.9 %all_to_all.66 = f32[4,1,1048576]{2,1,0:T(1,128)} all-to-all(f32[4,1,1048576]{2,1,0:T(1,128)} %reshape.410), channel_id=1, replica_groups=mesh['az'=4,'col'=8] {'az'}, dimensions={0} | all-to-all | bytes 33554432 | tf_op jit(solution)/shard_map/all_to_all | solution.py:133
  1804.7 54.6 %reduce = f32[4,1048576]{1,0:T(4,128)} reduce(f32[4,1,1048576]{2,1,0:T(1,128)} %all_to_all.66, f32[]{:T(128)} %broadcast.379), dimensions={1}, to_apply=%all_to_all.58.reduce_sub_computation | reduce | bytes 33554436 | tf_op jit(solution)/shard_map/all_to_all | solution.py:133
  1859.3 55.2 %reshape.411 = f32[2048,32,64]{2,1,0:T(8,128)} reshape(f32[4,1048576]{1,0:T(4,128)} %reduce) | data formatting | bytes 33554432
  1914.5 26.2 %copy.72 = f32[64,4,32,512]{3,2,1,0:T(8,128)} copy(f32[64,4,32,512]{0,2,3,1:T(8,128)} %bitcast.105) | data formatting | bytes 33554432 | tf_op jit(solution)/shard_map/all_to_all | solution.py:133
  (50 shorter events, 179.7 us)
Async XLA Ops:
  10.9 36.2 %collective-permute-start = (f32[64,128,1]{1,0,2:T(8,128)S(1)}, f32[64,128,1]{1,0,2:T(8,128)S(1)}, u32[]{:S(2)}, u32[]{:S(2)}) collective-permute-start(f32[64,128,1]{1,0,2:T(8,128)S(1)} %copy.82), channel_id=1, source_target_pairs={{0,8},{8,16},{16,24},{24,0},{1,9},{9,17},{17,25},{25,1},{2,10},{10... | collective-permute-start | bytes 98312 | tf_op jit(solution)/shard_map/ppermute | solution.py:19
  16.8 34.9 %collective-permute-start.1 = (f32[64,128,1]{1,0,2:T(8,128)S(1)}, f32[64,128,1]{1,0,2:T(8,128)S(1)}, u32[]{:S(2)}, u32[]{:S(2)}) collective-permute-start(f32[64,128,1]{1,0,2:T(8,128)S(1)} %copy.83), channel_id=1, source_target_pairs={{8,0},{16,8},{24,16},{0,24},{9,1},{17,9},{25,17},{1,25},{10,2},{18... | collective-permute-start | bytes 98312 | tf_op jit(solution)/shard_map/ppermute | solution.py:22
  57.3 6.7 collective-permute-start.2
  57.4 6.6 collective-permute-start.3
  150.2 9.9 copy-start.2
  150.2 372.9 %all-to-all-start = ((f32[2,64,128,512]{3,1,0,2:T(8,128)}), f32[2,64,128,512]{3,1,0,2:T(8,128)}, u32[]{:S(2)}, u32[]{:S(2)}) async-start(f32[2,64,128,512]{3,1,0,2:T(8,128)} %pad_maximum_fusion), calls=%async_computation | async-start | bytes 67108864 | tf_op jit(solution)/shard_map/all_to_all | solution.py:95
  160.2 400.8 %copy-start = (s32[512]{0:T(512)}, s32[512]{0:T(512)S(1)}, u32[]{:S(2)}) copy-start(s32[512]{0:T(512)S(1)} %reshape.391) | copy-start | bytes 6148
  745.4 368.6 %all-to-all-start.1 = ((f32[512,32,256]{2,1,0:T(8,128)}), f32[512,32,256]{2,1,0:T(8,128)}, u32[]{:S(2)}, u32[]{:S(2)}) async-start(f32[512,32,256]{2,1,0:T(8,128)} %copy.57), calls=%async_computation.1 | async-start | bytes 33554432 | tf_op jit(solution)/shard_map/all_to_all | solution.py:100
  1253.9 4.2 copy-start.1
  1253.9 189.1 %all-to-all-start.2 = ((f32[16,1024,128]{2,0,1:T(8,128)}), f32[16,1024,128]{2,0,1:T(8,128)}, u32[]{:S(2)}, u32[]{:S(2)}) async-start(f32[16,1024,128]{2,0,1:T(8,128)} %copy.67), calls=%async_computation.2 | async-start | bytes 16777216 | tf_op jit(solution)/shard_map/all_to_all | solution.py:129
where the time goes:
time: 1950 us; the launch traced here: 1940 us
  waiting for transfers between devices  855 us (44%)
  local copies, waits for them, and re-layouts  419 us (21%)
  matrix products  260 us (13%)
  blocking collectives  194 us (10%)
  other arithmetic  186 us (10%)
  starting transfers between devices  25.8 us (1%)
    all_to_all x1, waiting for transfers between devices, body(): lax.all_to_all(fields, 'az', split_axis=2, concat_axis=3, tiled=True)  345 us
    all_to_all x1, waiting for transfers between devices, body(): lax.all_to_all(spectra, ('az', 'col'), split_axis=0, concat_axis=1, tiled...  342 us
    all_to_all x1, blocking collectives, body(): lax.all_to_all(row_fields, 'az', split_axis=2, concat_axis=1, tiled=True)  194 us
    all_to_all x1, waiting for transfers between devices, body(): lax.all_to_all(synthesis, ('az', 'col'), split_axis=1, concat_axis=0, til...  166 us
    unnamed x15, local copies, waits for them, and re-layouts  153 us
    dot_general x1, matrix products, body(): jnp.einsum('frtp,pqk->ktqfr', lax.all_to_all(fields, 'az', split_axis=2,...  113 us
    all_to_all x2, local copies, waits for them, and re-layouts, body(): lax.all_to_all(fields, 'az', split_axis=2, concat_axis=3, tiled=True)  77.8 us
    dot_general x1, matrix products, body(): jnp.einsum('ktqr,qkp->rtp', grid_modes, inverse_table, precision=highest_...  67.6 us
  transfers between devices with their start and end apart: 7, of which 4 were waited for; matrix products, arithmetic and copies ran while one was open for 5% of the time, Pallas kernels for 0%

commit v1 on v0

v1 whole, which is shorter than its diff:
```python
import functools
import math

import jax
import jax.numpy as jnp
from jax import lax
from jax.experimental import pallas as pl
from jax.experimental.pallas import tpu as pltpu
from jax.sharding import PartitionSpec as P

step_time = 0.002
mobility_step = 4e-06
highest_precision = lax.Precision.HIGHEST
vmem_limit = 48 * 1024 * 1024
chunk_count = 4


def shell_radii(shells):
    return 0.75 + 0.25 * (jnp.arange(shells, dtype=jnp.float32) + 0.5) / shells


def colat_weights(count):
    row_index = jnp.arange(count, dtype=jnp.int32)
    waves = jnp.arange(1, count // 2 + 1, dtype=jnp.int32)
    turns = (2 * row_index[:, None] + 1) * waves[None, :] % (2 * count)
    cosines = jnp.cos(turns.astype(jnp.float32) * (math.pi / count))
    wave_float = waves.astype(jnp.float32)
    coefs = 1.0 / (4.0 * wave_float * wave_float - 1.0)
    return 2.0 / count * (1.0 - 2.0 * jnp.dot(cosines, coefs, precision=highest_precision))


def split_bf16(value):
    high = value.astype(jnp.bfloat16)
    low = (value - high.astype(jnp.float32)).astype(jnp.bfloat16)
    return high, low


def split_rounded(value):
    high = lax.reduce_precision(value, exponent_bits=8, mantissa_bits=7)
    return high.astype(jnp.bfloat16), (value - high).astype(jnp.bfloat16)


def dot_nt(a, b):
    return lax.dot_general(a, b, (((1,), (1,)), ((), ())), preferred_element_type=jnp.float32)


def dot_nn(a, b):
    return jnp.dot(a, b, preferred_element_type=jnp.float32)


def grid_kernel(shells, phi_count, theta_count, off_ref, c_ref, v_ref, rows_ref, cols_ref, o_ref):
    c = c_ref[0]
    theta_local, phi_local = c.shape
    lane = lax.broadcasted_iota(jnp.int32, c.shape, 1)
    row = lax.broadcasted_iota(jnp.int32, c.shape, 0)
    east = jnp.where(lane == phi_local - 1, cols_ref[0, :, 1:2], pltpu.roll(c, phi_local - 1, 1))
    west = jnp.where(lane == 0, cols_ref[0, :, 0:1], pltpu.roll(c, 1, 1))
    south = jnp.where(row == theta_local - 1, rows_ref[0, 1:2, :], pltpu.roll(c, theta_local - 1, 0))
    north = jnp.where(row == 0, rows_ref[0, 0:1, :], pltpu.roll(c, 1, 0))
    d_phi = (east - west) * (phi_count / (4.0 * math.pi))
    d_theta = (south - north) * (theta_count / (2.0 * math.pi))
    shell = jnp.full((1, 1), off_ref[0] + pl.program_id(0), jnp.int32).astype(jnp.float32)
    inverse_radius = 1.0 / (0.75 + 0.25 * (shell + 0.5) / shells)
    spin_rate = v_ref[0, 0].astype(jnp.float32)
    sweep_speed = v_ref[1, 0].astype(jnp.float32)
    o_ref[0, 0] = c - step_time * (spin_rate * d_phi + sweep_speed * inverse_radius * d_theta)
    o_ref[1, 0] = c * c * c - c


def grid_fields(phase_field, velocity, rows, cols, offset, count, phi_count, theta_count):
    shells, theta_local, phi_local = phase_field.shape
    return pl.pallas_call(
        functools.partial(grid_kernel, shells, phi_count, theta_count),
        grid_spec=pltpu.PrefetchScalarGridSpec(
            num_scalar_prefetch=1,
            grid=(count,),
            in_specs=[
                pl.BlockSpec((1, theta_local, phi_local), lambda i, off: (off[0] + i, 0, 0)),
                pl.BlockSpec((2, 1, theta_local, phi_local), lambda i, off: (0, off[0] + i, 0, 0)),
                pl.BlockSpec((1, 2, phi_local), lambda i, off: (off[0] + i, 0, 0)),
                pl.BlockSpec((1, theta_local, 2), lambda i, off: (off[0] + i, 0, 0)),
            ],
            out_specs=pl.BlockSpec((2, 1, theta_local, phi_local), lambda i, off: (0, i, 0, 0)),
        ),
        out_shape=jax.ShapeDtypeStruct((2, count, theta_local, phi_local), jnp.float32),
        compiler_params=pltpu.CompilerParams(vmem_limit_bytes=vmem_limit),
        cost_estimate=pl.CostEstimate(
            flops=20 * count * theta_local * phi_local,
            bytes_accessed=16 * count * theta_local * phi_local,
            transcendentals=0,
        ),
    )(offset.reshape(1), phase_field, velocity, rows, cols)


def forward_kernel(own_ref, other_ref, high_ref, low_ref, o_ref):
    _, block, theta_local, phi_local = own_ref.shape
    own = own_ref[0].reshape(block * theta_local, phi_local)
    other = other_ref[0].reshape(block * theta_local, phi_local)
    high, low = split_bf16(jnp.concatenate([own, other], axis=1))
    sums = dot_nt(high_ref[...], high) + dot_nt(high_ref[...], low) + dot_nt(low_ref[...], high)
    classes, cols, _, _, pairs, _ = o_ref.shape
    for j in range(block):
        part = sums[:, j * theta_local : (j + 1) * theta_local]
        o_ref[:, :, 0, j] = part.reshape(classes, cols, pairs, theta_local)


def forward_sums(own, other, high, low, cols, pairs):
    fields, count, theta_local, phi_local = own.shape
    rows = high.shape[0]
    classes = rows // (cols * pairs)
    block = 4
    field_spec = pl.BlockSpec((1, block, theta_local, phi_local), lambda f, i: (f, i, 0, 0))
    table_spec = pl.BlockSpec((rows, 2 * phi_local), lambda f, i: (0, 0))
    return pl.pallas_call(
        forward_kernel,
        grid=(fields, count // block),
        in_specs=[field_spec, field_spec, table_spec, table_spec],
        out_specs=pl.BlockSpec(
            (classes, cols, 1, block, pairs, theta_local), lambda f, i: (0, 0, f, i, 0, 0)
        ),
        out_shape=jax.ShapeDtypeStruct(
            (classes, cols, fields, count, pairs, theta_local), jnp.float32
        ),
        compiler_params=pltpu.CompilerParams(vmem_limit_bytes=vmem_limit),
        cost_estimate=pl.CostEstimate(
            flops=12 * rows * fields * count * theta_local * phi_local,
            bytes_accessed=8 * own.size + 4 * rows * fields * count * theta_local,
            transcendentals=0,
        ),
    )(own, other, high, low)


def inverse_kernel(here_ref, there_ref, high_ref, low_ref, keep_ref, send_ref):
    block, theta_local, phi_local = keep_ref.shape
    parts = []
    for j in range(block):
        here = here_ref[:, :, j].reshape(-1, theta_local)
        there = there_ref[:, :, j].reshape(-1, theta_local)
        parts.append(jnp.concatenate([here, there], axis=0).T)
    high, low = split_bf16(jnp.concatenate(parts, axis=0))
    values = dot_nn(high, high_ref[...]) + dot_nn(high, low_ref[...]) + dot_nn(low, high_ref[...])
    keep_ref[...] = values[:, :phi_local].reshape(block, theta_local, phi_local)
    send_ref[...] = values[:, phi_local:].reshape(block, theta_local, phi_local)


def inverse_sums(here, there, high, low):
    classes, cols, count, pairs, theta_local = here.shape
    rows, phi_two = high.shape
    block = 4
    half_spec = pl.BlockSpec(
        (classes, cols, block, pairs, theta_local), lambda i: (0, 0, i, 0, 0)
    )
    table_spec = pl.BlockSpec((rows, phi_two), lambda i: (0, 0))
    out_spec = pl.BlockSpec((block, theta_local, phi_two // 2), lambda i: (i, 0, 0))
    out_type = jax.ShapeDtypeStruct((count, theta_local, phi_two // 2), jnp.float32)
    return pl.pallas_call(
        inverse_kernel,
        grid=(count // block,),
        in_specs=[half_spec, half_spec, table_spec, table_spec],
        out_specs=[out_spec, out_spec],
        out_shape=[out_type, out_type],
        compiler_params=pltpu.CompilerParams(vmem_limit_bytes=vmem_limit),
        cost_estimate=pl.CostEstimate(
            flops=6 * rows * count * theta_local * phi_two,
            bytes_accessed=8 * here.size + 4 * count * theta_local * phi_two,
            transcendentals=0,
        ),
    )(here, there, high, low)


def swap_az(value, bit):
    count = lax.axis_size("az")
    return lax.ppermute(value, "az", [(i, i ^ (1 << bit)) for i in range(count)])


def body(phase_field, velocity, owned_modes, legendre, radial_inverse):
    shells, theta_local, phi_local = phase_field.shape
    az_count = lax.axis_size("az")
    col_count = lax.axis_size("col")
    az_here = lax.axis_index("az")
    col_here = lax.axis_index("col")
    bits = az_count.bit_length() - 1
    phi_count = phi_local * az_count
    theta_count = theta_local * col_count
    mode_dev, _, degree_count = legendre.shape
    pairs = 2 * mode_dev
    shell_radius = shell_radii(shells)

    east_going = [(i, (i + 1) % az_count) for i in range(az_count)]
    west_going = [(j, i) for i, j in east_going]
    south_going = [(i, i + 1) for i in range(col_count - 1)]
    north_going = [(j, i) for i, j in south_going]
    west_col = lax.ppermute(phase_field[:, :, phi_local - 1], "az", east_going)
    east_col = lax.ppermute(phase_field[:, :, 0], "az", west_going)
    north_row = lax.ppermute(phase_field[:, theta_local - 1, :], "col", south_going)
    south_row = lax.ppermute(phase_field[:, 0, :], "col", north_going)
    north_row = jnp.where(col_here == 0, 0.0, north_row)
    south_row = jnp.where(col_here == col_count - 1, 0.0, south_row)
    rows = jnp.stack([north_row, south_row], axis=1)
    cols = jnp.stack([west_col, east_col], axis=2)

    mode_table = owned_modes.reshape(az_count, col_count * mode_dev)
    local_phi = jnp.arange(phi_local, dtype=jnp.int32)

    def tables(pair_bit):
        rest = [k for k in range(bits) if k != pair_bit]
        order = [0, 1 << pair_bit]
        for k in reversed(rest):
            order = order + [d | (1 << k) for d in order]
        modes = jnp.concatenate(
            [lax.dynamic_index_in_dim(mode_table, az_here ^ d, 0, keepdims=False) for d in order]
        )
        phi = jnp.concatenate(
            [az_here * phi_local + local_phi, (az_here ^ (1 << pair_bit)) * phi_local + local_phi]
        )
        turns = modes[:, None, None] * phi[None, None, :] % phi_count
        quarter = jnp.arange(2, dtype=jnp.int32)[None, :, None] * (phi_count // 4)
        turns = (turns + quarter) % phi_count
        wave = jnp.cos(turns.astype(jnp.float32) * (2.0 * math.pi / phi_count))
        wave = wave.reshape(2 * modes.shape[0], 2 * phi_local)
        high, low = split_rounded(wave)
        gain = jnp.where(modes == 0, 1.0, 2.0).astype(jnp.bfloat16)
        gain = jnp.repeat(gain, 2)[:, None]
        scale = jnp.bfloat16(1.0 / phi_count)
        return rest, (high * scale, low * scale), (high * gain, low * gain)

    pair_bits = [j % bits for j in range(chunk_count)]
    plans = {b: tables(b) for b in sorted(set(pair_bits))}

    chunk = shells // chunk_count
    half = chunk // 2
    weights = colat_weights(theta_count)
    degrees = jnp.arange(degree_count, dtype=jnp.float32)
    degree_factor = degrees * (degrees + 1.0)

    def to_cols(value):
        return lax.all_to_all(value, "col", split_axis=0, concat_axis=0, tiled=True)

    right_sides = []
    for j, b in enumerate(pair_bits):
        rest, (high, low), _ = plans[b]
        mine = (az_here >> b) & 1
        make = functools.partial(
            grid_fields, phase_field, velocity, rows, cols,
            count=half, phi_count=phi_count, theta_count=theta_count,
        )
        other = swap_az(make(offset=j * chunk + (1 - mine) * half), b)
        own = make(offset=j * chunk + mine * half)
        cut = high.shape[0] // 2
        sums = swap_az(forward_sums(own, other, high[cut:], low[cut:], col_count, pairs), rest[0])
        sums = sums + forward_sums(own, other, high[:cut], low[:cut], col_count, pairs)
        for k in rest[1:]:
            middle = sums.shape[0] // 2
            sums = sums[:middle] + swap_az(sums[middle:], k)
        mine_half = to_cols(sums[0])
        other_half = to_cols(swap_az(sums[1], b))
        first = jnp.where(mine == 0, mine_half, other_half)
        second = jnp.where(mine == 0, other_half, mine_half)
        both = jnp.concatenate([first, second], axis=2)
        both = both.reshape(col_count, 2, chunk, mode_dev, 2, theta_local)
        both = jnp.transpose(both, (3, 1, 4, 2, 0, 5))
        both = both.reshape(mode_dev, 4 * chunk, theta_count) * weights
        lhs = jnp.concatenate(split_rounded(both), axis=1)
        coeffs = jnp.einsum("qxt,qtl->qxl", lhs, legendre, preferred_element_type=jnp.float32)
        coeffs = coeffs[:, : 4 * chunk] + coeffs[:, 4 * chunk :]
        coeffs = coeffs.reshape(mode_dev, 2, 2, chunk, degree_count)
        radius = shell_radius[j * chunk : (j + 1) * chunk]
        factor = mobility_step * degree_factor[None, :] / (radius * radius)[:, None]
        right_sides.append(coeffs[:, 0] - factor * coeffs[:, 1])

    right_side = jnp.concatenate(right_sides, axis=2)
    right_side = jnp.transpose(right_side, (3, 2, 0, 1)).reshape(degree_count, shells, pairs)
    rhs = jnp.concatenate(split_rounded(right_side), axis=2)
    solved = jnp.einsum("lrs,lsn->lrn", radial_inverse, rhs, preferred_element_type=jnp.float32)
    solved = solved[:, :, :pairs] + solved[:, :, pairs:]
    solved = jnp.transpose(solved.reshape(degree_count, shells, mode_dev, 2), (2, 1, 3, 0))

    pieces = []
    for j, b in enumerate(pair_bits):
        rest, _, (high, low) = plans[b]
        mine = (az_here >> b) & 1
        part = solved[:, j * chunk : (j + 1) * chunk].reshape(mode_dev, 2 * chunk, degree_count)
        lhs = jnp.concatenate(split_rounded(part), axis=1)
        grid_modes = jnp.einsum("qxl,qtl->qxt", lhs, legendre, preferred_element_type=jnp.float32)
        grid_modes = grid_modes[:, : 2 * chunk] + grid_modes[:, 2 * chunk :]
        grid_modes = grid_modes.reshape(mode_dev, 2, half, 2, col_count, theta_local)
        grid_modes = jnp.transpose(grid_modes, (1, 4, 2, 0, 3, 5))
        grid_modes = grid_modes.reshape(2, col_count, half, pairs, theta_local)
        keep_half = to_cols(jnp.where(mine == 0, grid_modes[0], grid_modes[1]))
        send_half = swap_az(to_cols(jnp.where(mine == 0, grid_modes[1], grid_modes[0])), b)
        here = jnp.stack([keep_half, send_half])
        there = None
        for k in reversed(rest):
            if there is not None:
                here = jnp.concatenate([here, there])
            there = swap_az(here, k)
        keep, send = inverse_sums(here, there, high, low)
        arrived = swap_az(send, b)
        pieces.append(jnp.where(mine == 0, keep, arrived))
        pieces.append(jnp.where(mine == 0, arrived, keep))
    return jnp.concatenate(pieces, axis=0)


def solution(mesh):
    in_specs = (
        P(None, "col", "az"),
        P(None, None, "col", "az"),
        P(),
        P(("az", "col"), None, None),
        P(),
    )
    out_specs = P(None, "col", "az")
    return jax.shard_map(body, mesh=mesh, in_specs=in_specs, out_specs=out_specs, check_vma=False)
```

time: 1950 us -> 1460 us (0.75)
  waiting for transfers between devices: 855 us -> 649 us
  local copies, waits for them, and re-layouts: 419 us -> 214 us
  Pallas kernels: 0 us -> 175 us
  matrix products: 260 us -> 106 us
  blocking collectives: 194 us -> 58.7 us
  starting transfers between devices: 25.8 us -> 95.8 us
  other arithmetic: 186 us -> 154 us
    all_to_all x3 -> x14, waiting for transfers between devices: 852 us -> 63.6 us  [to_cols(): return lax.all_to_all(value, 'col', split_axis=0, concat_axis=0, tiled=True)]
    ppermute x4 -> x28, waiting for transfers between devices: 2.9 us -> 586 us  [the longest x24 585 us: swap_az(): return lax.ppermute(value, 'az', [(i, i ^ 1 << bit) for i in range(count)])]
    pallas_call x0 -> x20, Pallas kernels: none -> 175 us  [the longest x8 80.3 us: forward_sums(): pl.pallas_call(forward_kernel, grid=(fields, count // block), in_specs=[f...]
    dot_general x5 -> x9, matrix products: 250 us -> 96.5 us  [the longest x4 51.7 us: body(): jnp.einsum('qxl,qtl->qxt', lhs, legendre, preferred_element_type=jnp.floa...]
    all_to_all x1 -> x2, blocking collectives: 194 us -> 58.7 us  [to_cols(): return lax.all_to_all(value, 'col', split_axis=0, concat_axis=0, tiled=True)]
    unnamed x15 -> x52, local copies, waits for them, and re-layouts: 153 us -> 36.1 us
    all_to_all x5 -> x0, local copies, waits for them, and re-layouts: 115 us -> none  [the longest x2 77.8 us: body(): lax.all_to_all(fields, 'az', split_axis=2, concat_axis=3, tiled=True)]
    slice x3 -> x11, local copies, waits for them, and re-layouts: 28.3 us -> 86.5 us  [the longest x5 74.6 us: body(): solved[:, j * chunk:(j + 1) * chunk]]
  transfers between devices with their start and end apart: 7 -> 42, of which waited for: 4 -> 24; matrix products, arithmetic and copies ran while one was open for 5% -> 19% of each run, Pallas kernels for 0% -> 12%
where the time goes in v1:
time: 1460 us; the launch traced here: 1450 us
  waiting for transfers between devices  649 us (44%)
  local copies, waits for them, and re-layouts  214 us (15%)
  Pallas kernels  175 us (12%)
  other arithmetic  154 us (11%)
  matrix products  106 us (7%)
  starting transfers between devices  95.8 us (7%)
  blocking collectives  58.7 us (4%)
    ppermute x24, waiting for transfers between devices, swap_az(): return lax.ppermute(value, 'az', [(i, i ^ 1 << bit) for i in range(count)])  585 us
    pallas_call x8, Pallas kernels, forward_sums(): pl.pallas_call(forward_kernel, grid=(fields, count // block), in_specs=[f...  80.3 us
    slice x5, local copies, waits for them, and re-layouts, body(): solved[:, j * chunk:(j + 1) * chunk]  74.6 us
    all_to_all x14, starting transfers between devices, to_cols(): return lax.all_to_all(value, 'col', split_axis=0, concat_axis=0, tiled=True)  68.4 us
    all_to_all x14, waiting for transfers between devices, to_cols(): return lax.all_to_all(value, 'col', split_axis=0, concat_axis=0, tiled=True)  63.6 us
    all_to_all x2, blocking collectives, to_cols(): return lax.all_to_all(value, 'col', split_axis=0, concat_axis=0, tiled=True)  58.7 us
    pallas_call x8, Pallas kernels, grid_fields(): pl.pallas_call(functools.partial(grid_kernel, shells, phi_count, theta_co...  54.7 us
    dot_general x4, matrix products, body(): jnp.einsum('qxl,qtl->qxt', lhs, legendre, preferred_element_type=jnp.floa...  51.7 us
  transfers between devices with their start and end apart: 42, of which 24 were waited for; matrix products, arithmetic and copies ran while one was open for 19% of the time, Pallas kernels for 12%

profile of v1, /device:TPU:0, one launch (start us, length us, event | category | flops | bytes accessed | tf_op | source)
XLA Modules:
  0.0 1454.3 jit_solution(14664086404398222496)
XLA Ops:
  57.7 36.6 %broadcast_multiply_fusion.2 = (bf16[1024,1024]{1,0:T(8,128)(2,1)}, f32[1024,1024]{1,0:T(8,128)}, bf16[1024,1024]{1,0:T(8,128)(2,1)}, f32[1024,1024]{1,0:T(8,128)S(1)}) fusion(bf16[1024]{0:T(1024)(128)(2,1)S(1)} %mul.331, s32[1024,1024]{1,0:T(8,128)} %add.243, s32[1024]{0:T(1024)S(1)} %add.245, bf16[1024]{0:T(1024)(128)(2,1)S(1)} %mul.335, ...), kind=kLoop, calls=%fused_computation.164 | loop fusion | flops 44040192 | bytes 20979712 | tf_op jit(solution)/shard_map/mul | solution.py:225
  159.5 35.8 %collective-permute-done.10.other_ref = f32[2,8,128,512]{3,2,1,0:T(8,128)} collective-permute-done((f32[2,8,128,512]{3,2,1,0:T(8,128)}, f32[2,8,128,512]{3,2,1,0:T(8,128)}, u32[]{:S(2)}, u32[]{:S(2)}) %collective-permute-start.10) | collective-permute-done | bytes 4194336 | tf_op jit(solution)/shard_map/ppermute | solution.py:173
  215.8 69.4 %collective-permute-done.14 = f32[2,8,2,8,32,128]{5,4,3,2,1,0:T(8,128)} collective-permute-done((f32[2,8,2,8,32,128]{5,4,3,2,1,0:T(8,128)}, f32[2,8,2,8,32,128]{5,4,3,2,1,0:T(8,128)}, u32[]{:S(2)}, u32[]{:S(2)}) %collective-permute-start.14) | collective-permute-done | bytes 4194336 | tf_op jit(solution)/shard_map/ppermute | solution.py:173
  362.7 39.5 %collective-permute-done.4.other_ref = f32[2,8,128,512]{3,2,1,0:T(8,128)} collective-permute-done((f32[2,8,128,512]{3,2,1,0:T(8,128)}, f32[2,8,128,512]{3,2,1,0:T(8,128)}, u32[]{:S(2)}, u32[]{:S(2)}) %collective-permute-start.4) | collective-permute-done | bytes 4194336 | tf_op jit(solution)/shard_map/ppermute | solution.py:173
  422.8 69.0 %collective-permute-done.8 = f32[2,8,2,8,32,128]{5,4,3,2,1,0:T(8,128)} collective-permute-done((f32[2,8,2,8,32,128]{5,4,3,2,1,0:T(8,128)}, f32[2,8,2,8,32,128]{5,4,3,2,1,0:T(8,128)}, u32[]{:S(2)}, u32[]{:S(2)}) %collective-permute-start.8) | collective-permute-done | bytes 4194336 | tf_op jit(solution)/shard_map/ppermute | solution.py:173
  520.7 32.1 %all-to-all-done.2 = f32[8,2,8,32,128]{4,3,2,1,0:T(8,128)} async-done(((f32[8,2,8,32,128]{4,3,2,1,0:T(8,128)}), f32[8,2,8,32,128]{4,3,2,1,0:T(8,128)}, u32[]{:S(2)}, u32[]{:S(2)}) %all-to-all-start.2) | async-done | bytes 2097184 | tf_op jit(solution)/shard_map/all_to_all | solution.py:237
  557.0 47.7 %collective-permute-done.15 = f32[8,2,8,32,128]{4,3,2,1,0:T(8,128)} collective-permute-done((f32[8,2,8,32,128]{4,3,2,1,0:T(8,128)}, f32[8,2,8,32,128]{4,3,2,1,0:T(8,128)}, u32[]{:S(2)}, u32[]{:S(2)}) %collective-permute-start.15) | collective-permute-done | bytes 2097184 | tf_op jit(solution)/shard_map/ppermute | solution.py:173
  610.4 47.6 %collective-permute-done.12 = f32[8,2,8,32,128]{4,3,2,1,0:T(8,128)} collective-permute-done((f32[8,2,8,32,128]{4,3,2,1,0:T(8,128)}, f32[8,2,8,32,128]{4,3,2,1,0:T(8,128)}, u32[]{:S(2)}, u32[]{:S(2)}) %collective-permute-start.12) | collective-permute-done | bytes 2097184 | tf_op jit(solution)/shard_map/ppermute | solution.py:173
  663.8 47.7 %collective-permute-done.9 = f32[8,2,8,32,128]{4,3,2,1,0:T(8,128)} collective-permute-done((f32[8,2,8,32,128]{4,3,2,1,0:T(8,128)}, f32[8,2,8,32,128]{4,3,2,1,0:T(8,128)}, u32[]{:S(2)}, u32[]{:S(2)}) %collective-permute-start.9) | collective-permute-done | bytes 2097184 | tf_op jit(solution)/shard_map/ppermute | solution.py:173
  717.3 47.6 %collective-permute-done.6 = f32[8,2,8,32,128]{4,3,2,1,0:T(8,128)} collective-permute-done((f32[8,2,8,32,128]{4,3,2,1,0:T(8,128)}, f32[8,2,8,32,128]{4,3,2,1,0:T(8,128)}, u32[]{:S(2)}, u32[]{:S(2)}) %collective-permute-start.6) | collective-permute-done | bytes 2097184 | tf_op jit(solution)/shard_map/ppermute | solution.py:173
  770.1 13.0 copy.87
  940.1 33.6 %fusion.105 = (f32[16,16,2,512]{1,2,0,3:T(2,128)}, f32[16,16,2,512]{1,2,0,3:T(2,128)}, f32[16,16,2,512]{1,2,0,3:T(2,128)}, f32[16,16,2,512]{1,2,0,3:T(2,128)}) fusion(f32[16,64,2,512]{1,2,0,3:T(2,128)} %bitcast.186), kind=kLoop, calls=%fused_computation.252 | loop fusion | bytes 8388608 | tf_op jit(solution)/shard_map/slice | solution.py:282
  985.1 12.9 fusion.69
  1057.9 15.7 %all-to-all-done.13 = f32[8,8,32,128]{3,2,1,0:T(8,128)S(1)} async-done(((f32[8,8,32,128]{3,2,1,0:T(8,128)}), f32[8,8,32,128]{3,2,1,0:T(8,128)S(1)}, u32[]{:S(2)}, u32[]{:S(2)}) %all-to-all-start.13) | async-done | bytes 1048608 | tf_op jit(solution)/shard_map/all_to_all | solution.py:237
  1078.2 12.9 fusion.61
  1115.7 12.9 fusion.57
  1142.1 29.7 %all_to_all.80 = f32[8,8,32,128]{3,2,1,0:T(8,128)} all-to-all(f32[8,8,32,128]{3,2,1,0:T(8,128)S(1)} %bitcast.209), channel_id=1, replica_groups=mesh['az'=4,'col'=8] {'col'}, dimensions={0} | all-to-all | bytes 2097152 | tf_op jit(solution)/shard_map/all_to_all | solution.py:237
  1171.8 29.0 %all_to_all.81 = f32[8,8,32,128]{3,2,1,0:T(8,128)S(1)} all-to-all(f32[8,8,32,128]{3,2,1,0:T(8,128)S(1)} %bitcast.208), channel_id=1, replica_groups=mesh['az'=4,'col'=8] {'col'}, dimensions={0} | all-to-all | bytes 2097152 | tf_op jit(solution)/shard_map/all_to_all | solution.py:237
  1205.6 24.5 %collective-permute-done.16 = f32[8,8,32,128]{3,2,1,0:T(8,128)S(1)} collective-permute-done((f32[8,8,32,128]{3,2,1,0:T(8,128)}, f32[8,8,32,128]{3,2,1,0:T(8,128)S(1)}, u32[]{:S(2)}, u32[]{:S(2)}) %collective-permute-start.16) | collective-permute-done | bytes 1048608 | tf_op jit(solution)/shard_map/ppermute | solution.py:173
  1243.7 19.8 %collective-permute-done.22 = f32[8,8,32,128]{3,2,1,0:T(8,128)S(1)} collective-permute-done((f32[8,8,32,128]{3,2,1,0:T(8,128)}, f32[8,8,32,128]{3,2,1,0:T(8,128)S(1)}, u32[]{:S(2)}, u32[]{:S(2)}) %collective-permute-start.22) | collective-permute-done | bytes 1048608 | tf_op jit(solution)/shard_map/ppermute | solution.py:173
  1266.5 36.5 %collective-permute-done.25 = f32[8,8,32,128]{3,2,1,0:T(8,128)} collective-permute-done((f32[8,8,32,128]{3,2,1,0:T(8,128)}, f32[8,8,32,128]{3,2,1,0:T(8,128)}, u32[]{:S(2)}, u32[]{:S(2)}) %collective-permute-start.25) | collective-permute-done | bytes 1048608 | tf_op jit(solution)/shard_map/ppermute | solution.py:173
  1328.1 19.8 %collective-permute-done.23.there_ref = f32[2,8,8,32,128]{4,3,2,1,0:T(8,128)} collective-permute-done((f32[2,8,8,32,128]{4,3,2,1,0:T(8,128)S(1)}, f32[2,8,8,32,128]{4,3,2,1,0:T(8,128)}, u32[]{:S(2)}, u32[]{:S(2)}) %collective-permute-start.23) | collective-permute-done | bytes 2097184 | tf_op jit(solution)/shard_map/ppermute | solution.py:173
  1370.0 29.6 %collective-permute-done.18 = f32[8,128,512]{2,1,0:T(8,128)} collective-permute-done((f32[8,128,512]{2,1,0:T(8,128)S(1)}, f32[8,128,512]{2,1,0:T(8,128)}, u32[]{:S(2)}, u32[]{:S(2)}) %collective-permute-start.18) | collective-permute-done | bytes 2097184 | tf_op jit(solution)/shard_map/ppermute | solution.py:173
  1404.7 38.2 %collective-permute-done.24 = f32[8,128,512]{2,1,0:T(8,128)} collective-permute-done((f32[8,128,512]{2,1,0:T(8,128)}, f32[8,128,512]{2,1,0:T(8,128)}, u32[]{:S(2)}, u32[]{:S(2)}) %collective-permute-start.24) | collective-permute-done | bytes 2097184 | tf_op jit(solution)/shard_map/ppermute | solution.py:173
  (262 shorter events, 652.1 us)
Async XLA Ops:
  34.4 91.1 %collective-permute-start.13 = (f32[2,8,128,512]{3,2,1,0:T(8,128)}, f32[2,8,128,512]{3,2,1,0:T(8,128)}, u32[]{:S(2)}, u32[]{:S(2)}) collective-permute-start(f32[2,8,128,512]{3,2,1,0:T(8,128)} %shard_map.68), channel_id=1, source_target_pairs={{0,16},{8,24},{16,0},{24,8},{1,17},{9,25},{17,1},{25,9},{2,18},{10... | collective-permute-start | bytes 12582920 | tf_op jit(solution)/shard_map/ppermute | solution.py:173
  103.9 91.4 %collective-permute-start.10 = (f32[2,8,128,512]{3,2,1,0:T(8,128)}, f32[2,8,128,512]{3,2,1,0:T(8,128)}, u32[]{:S(2)}, u32[]{:S(2)}) collective-permute-start(f32[2,8,128,512]{3,2,1,0:T(8,128)} %shard_map.64), channel_id=1, source_target_pairs={{0,8},{8,0},{16,24},{24,16},{1,9},{9,1},{17,25},{25,17},{2,10},{10... | collective-permute-start | bytes 12582920 | tf_op jit(solution)/shard_map/ppermute | solution.py:173
  135.7 149.5 %collective-permute-start.14 = (f32[2,8,2,8,32,128]{5,4,3,2,1,0:T(8,128)}, f32[2,8,2,8,32,128]{5,4,3,2,1,0:T(8,128)}, u32[]{:S(2)}, u32[]{:S(2)}) collective-permute-start(f32[2,8,2,8,32,128]{5,4,3,2,1,0:T(8,128)} %shard_map.69), channel_id=1, source_target_pairs={{0,8},{8,0},{16,24},{24,16},{1,9},{9,1},{17,25},{25,17},{2,10},{10... | collective-permute-start | bytes 12582920 | tf_op jit(solution)/shard_map/ppermute | solution.py:173
  148.1 169.1 %collective-permute-start.7 = (f32[2,8,128,512]{3,2,1,0:T(8,128)}, f32[2,8,128,512]{3,2,1,0:T(8,128)}, u32[]{:S(2)}, u32[]{:S(2)}) collective-permute-start(f32[2,8,128,512]{3,2,1,0:T(8,128)} %shard_map.60), channel_id=1, source_target_pairs={{0,16},{8,24},{16,0},{24,8},{1,17},{9,25},{17,1},{25,9},{2,18},{10... | collective-permute-start | bytes 12582920 | tf_op jit(solution)/shard_map/ppermute | solution.py:173
  205.3 133.4 %collective-permute-start.11 = (f32[2,8,2,8,32,128]{5,4,3,2,1,0:T(8,128)}, f32[2,8,2,8,32,128]{5,4,3,2,1,0:T(8,128)}, u32[]{:S(2)}, u32[]{:S(2)}) collective-permute-start(f32[2,8,2,8,32,128]{5,4,3,2,1,0:T(8,128)} %shard_map.65), channel_id=1, source_target_pairs={{0,16},{8,24},{16,0},{24,8},{1,17},{9,25},{17,1},{25,9},{2,18},{10... | collective-permute-start | bytes 12582920 | tf_op jit(solution)/shard_map/ppermute | solution.py:173
  292.1 58.1 %all-to-all-start.6 = ((f32[8,2,8,32,128]{4,3,2,1,0:T(8,128)}), f32[8,2,8,32,128]{4,3,2,1,0:T(8,128)}, u32[]{:S(2)}, u32[]{:S(2)}) async-start(f32[8,2,8,32,128]{4,3,2,1,0:T(8,128)} %get-tuple-element.63), calls=%async_computation.6 | async-start | bytes 4194304 | tf_op jit(solution)/shard_map/all_to_all | solution.py:237
  308.5 93.7 %collective-permute-start.4 = (f32[2,8,128,512]{3,2,1,0:T(8,128)}, f32[2,8,128,512]{3,2,1,0:T(8,128)}, u32[]{:S(2)}, u32[]{:S(2)}) collective-permute-start(f32[2,8,128,512]{3,2,1,0:T(8,128)} %shard_map.56), channel_id=1, source_target_pairs={{0,8},{8,0},{16,24},{24,16},{1,9},{9,1},{17,25},{25,17},{2,10},{10... | collective-permute-start | bytes 12582920 | tf_op jit(solution)/shard_map/ppermute | solution.py:173
  327.3 164.4 %collective-permute-start.8 = (f32[2,8,2,8,32,128]{5,4,3,2,1,0:T(8,128)}, f32[2,8,2,8,32,128]{5,4,3,2,1,0:T(8,128)}, u32[]{:S(2)}, u32[]{:S(2)}) collective-permute-start(f32[2,8,2,8,32,128]{5,4,3,2,1,0:T(8,128)} %shard_map.61), channel_id=1, source_target_pairs={{0,8},{8,0},{16,24},{24,16},{1,9},{9,1},{17,25},{25,17},{2,10},{10... | collective-permute-start | bytes 12582920 | tf_op jit(solution)/shard_map/ppermute | solution.py:173
  350.2 148.4 %all-to-all-start.4 = ((f32[8,2,8,32,128]{4,3,2,1,0:T(8,128)}), f32[8,2,8,32,128]{4,3,2,1,0:T(8,128)}, u32[]{:S(2)}, u32[]{:S(2)}) async-start(f32[8,2,8,32,128]{4,3,2,1,0:T(8,128)} %get-tuple-element.59), calls=%async_computation.4 | async-start | bytes 4194304 | tf_op jit(solution)/shard_map/all_to_all | solution.py:237
  412.2 101.5 %collective-permute-start.5 = (f32[2,8,2,8,32,128]{5,4,3,2,1,0:T(8,128)}, f32[2,8,2,8,32,128]{5,4,3,2,1,0:T(8,128)}, u32[]{:S(2)}, u32[]{:S(2)}) collective-permute-start(f32[2,8,2,8,32,128]{5,4,3,2,1,0:T(8,128)} %shard_map.57), channel_id=1, source_target_pairs={{0,16},{8,24},{16,0},{24,8},{1,17},{9,25},{17,1},{25,9},{2,18},{10... | collective-permute-start | bytes 12582920 | tf_op jit(solution)/shard_map/ppermute | solution.py:173
  498.6 54.2 %all-to-all-start.2 = ((f32[8,2,8,32,128]{4,3,2,1,0:T(8,128)}), f32[8,2,8,32,128]{4,3,2,1,0:T(8,128)}, u32[]{:S(2)}, u32[]{:S(2)}) async-start(f32[8,2,8,32,128]{4,3,2,1,0:T(8,128)} %get-tuple-element.55), calls=%async_computation.2 | async-start | bytes 4194304 | tf_op jit(solution)/shard_map/all_to_all | solution.py:237
  605.4 53.4 %all-to-all-start.7 = ((f32[8,2,8,32,128]{4,3,2,1,0:T(8,128)}), f32[8,2,8,32,128]{4,3,2,1,0:T(8,128)}, u32[]{:S(2)}, u32[]{:S(2)}) async-start(f32[8,2,8,32,128]{4,3,2,1,0:T(8,128)} %collective-permute-done.15), calls=%async_computation.7 | async-start | bytes 4194304 | tf_op jit(solution)/shard_map/all_to_all | solution.py:237
  658.8 53.4 %all-to-all-start.5 = ((f32[8,2,8,32,128]{4,3,2,1,0:T(8,128)}), f32[8,2,8,32,128]{4,3,2,1,0:T(8,128)}, u32[]{:S(2)}, u32[]{:S(2)}) async-start(f32[8,2,8,32,128]{4,3,2,1,0:T(8,128)} %collective-permute-done.12), calls=%async_computation.5 | async-start | bytes 4194304 | tf_op jit(solution)/shard_map/all_to_all | solution.py:237
  712.2 53.4 %all-to-all-start.3 = ((f32[8,2,8,32,128]{4,3,2,1,0:T(8,128)}), f32[8,2,8,32,128]{4,3,2,1,0:T(8,128)}, u32[]{:S(2)}, u32[]{:S(2)}) async-start(f32[8,2,8,32,128]{4,3,2,1,0:T(8,128)} %collective-permute-done.9), calls=%async_computation.3 | async-start | bytes 4194304 | tf_op jit(solution)/shard_map/all_to_all | solution.py:237
  765.7 66.0 %all-to-all-start.1 = ((f32[8,2,8,32,128]{4,3,2,1,0:T(8,128)}), f32[8,2,8,32,128]{4,3,2,1,0:T(8,128)}, u32[]{:S(2)}, u32[]{:S(2)}) async-start(f32[8,2,8,32,128]{4,3,2,1,0:T(8,128)} %collective-permute-done.6), calls=%async_computation.1 | async-start | bytes 4194304 | tf_op jit(solution)/shard_map/all_to_all | solution.py:237
  1231.6 74.7 %collective-permute-start.17 = (f32[2,8,8,32,128]{4,3,2,1,0:T(8,128)}, f32[2,8,8,32,128]{4,3,2,1,0:T(8,128)}, u32[]{:S(2)}, u32[]{:S(2)}) collective-permute-start(f32[2,8,8,32,128]{4,3,2,1,0:T(8,128)} %pad_maximum_fusion.4.here_ref), channel_id=1, source_target_pairs={{0,16},{8,24},{16,0},{24,8},{1,17},{9,25},{17,1},{25,9},{2,18},{10... | collective-permute-start | bytes 6291464 | tf_op jit(solution)/shard_map/ppermute | solution.py:173
  1240.7 77.0 %collective-permute-start.20 = (f32[2,8,8,32,128]{4,3,2,1,0:T(8,128)}, f32[2,8,8,32,128]{4,3,2,1,0:T(8,128)}, u32[]{:S(2)}, u32[]{:S(2)}) collective-permute-start(f32[2,8,8,32,128]{4,3,2,1,0:T(8,128)} %pad_maximum_fusion.5.here_ref), channel_id=1, source_target_pairs={{0,8},{8,0},{16,24},{24,16},{1,9},{9,1},{17,25},{25,17},{2,10},{10... | collective-permute-start | bytes 6291464 | tf_op jit(solution)/shard_map/ppermute | solution.py:173
  1242.1 60.8 %collective-permute-start.25 = (f32[8,8,32,128]{3,2,1,0:T(8,128)}, f32[8,8,32,128]{3,2,1,0:T(8,128)}, u32[]{:S(2)}, u32[]{:S(2)}) collective-permute-start(f32[8,8,32,128]{3,2,1,0:T(8,128)} %all-to-all-done.15), channel_id=1, source_target_pairs={{0,16},{8,24},{16,0},{24,8},{1,17},{9,25},{17,1},{25,9},{2,18},{10... | collective-permute-start | bytes 3145736 | tf_op jit(solution)/shard_map/ppermute | solution.py:173
  1264.9 83.0 %collective-permute-start.23 = (f32[2,8,8,32,128]{4,3,2,1,0:T(8,128)S(1)}, f32[2,8,8,32,128]{4,3,2,1,0:T(8,128)}, u32[]{:S(2)}, u32[]{:S(2)}) collective-permute-start(f32[2,8,8,32,128]{4,3,2,1,0:T(8,128)S(1)} %pad_maximum_fusion.6.here_ref), channel_id=1, source_target_pairs={{0,16},{8,24},{16,0},{24,8},{1,17},{9,25},{17,1},{25,9},{2,18},{10... | collective-permute-start | bytes 6291464 | tf_op jit(solution)/shard_map/ppermute | solution.py:173
  1305.8 53.5 %collective-permute-start.26 = (f32[2,8,8,32,128]{4,3,2,1,0:T(8,128)}, f32[2,8,8,32,128]{4,3,2,1,0:T(8,128)}, u32[]{:S(2)}, u32[]{:S(2)}) collective-permute-start(f32[2,8,8,32,128]{4,3,2,1,0:T(8,128)} %pad_maximum_fusion.7.here_ref), channel_id=1, source_target_pairs={{0,8},{8,0},{16,24},{24,16},{1,9},{9,1},{17,25},{25,17},{2,10},{10... | collective-permute-start | bytes 6291464 | tf_op jit(solution)/shard_map/ppermute | solution.py:173
  1316.2 83.4 %collective-permute-start.18 = (f32[8,128,512]{2,1,0:T(8,128)S(1)}, f32[8,128,512]{2,1,0:T(8,128)}, u32[]{:S(2)}, u32[]{:S(2)}) collective-permute-start(f32[8,128,512]{2,1,0:T(8,128)S(1)} %get-tuple-element.14), channel_id=1, source_target_pairs={{0,8},{8,0},{16,24},{24,16},{1,9},{9,1},{17,25},{25,17},{2,10},{10... | collective-permute-start | bytes 6291464 | tf_op jit(solution)/shard_map/ppermute | solution.py:173
  1327.5 74.7 %collective-permute-start.21 = (f32[8,128,512]{2,1,0:T(8,128)S(1)}, f32[8,128,512]{2,1,0:T(8,128)}, u32[]{:S(2)}, u32[]{:S(2)}) collective-permute-start(f32[8,128,512]{2,1,0:T(8,128)S(1)} %get-tuple-element.16), channel_id=1, source_target_pairs={{0,16},{8,24},{16,0},{24,8},{1,17},{9,25},{17,1},{25,9},{2,18},{10... | collective-permute-start | bytes 6291464 | tf_op jit(solution)/shard_map/ppermute | solution.py:173
  1358.7 84.2 %collective-permute-start.24 = (f32[8,128,512]{2,1,0:T(8,128)}, f32[8,128,512]{2,1,0:T(8,128)}, u32[]{:S(2)}, u32[]{:S(2)}) collective-permute-start(f32[8,128,512]{2,1,0:T(8,128)} %get-tuple-element.18), channel_id=1, source_target_pairs={{0,8},{8,0},{16,24},{24,16},{1,9},{9,1},{17,25},{25,17},{2,10},{10... | collective-permute-start | bytes 6291464 | tf_op jit(solution)/shard_map/ppermute | solution.py:173
  1369.4 76.1 %collective-permute-start.27 = (f32[8,128,512]{2,1,0:T(8,128)S(1)}, f32[8,128,512]{2,1,0:T(8,128)S(1)}, u32[]{:S(2)}, u32[]{:S(2)}) collective-permute-start(f32[8,128,512]{2,1,0:T(8,128)S(1)} %get-tuple-element.20), channel_id=1, source_target_pairs={{0,16},{8,24},{16,0},{24,8},{1,17},{9,25},{17,1},{25,9},{2,18},{10... | collective-permute-start | bytes 6291464 | tf_op jit(solution)/shard_map/ppermute | solution.py:173
  (39 other events, 924.6 us)
